TPU v7x, 32 devices: a whole 2x2x4 slice. The times are simulated.
32 devices in a mesh: branch: 4 (over y, x), seq: 8 (over z, core).
Axes of the slice: x: 2, y: 2, z: 4, core: 2. Of those that a mesh axis runs over, the one named last changes fastest.
Arguments:
- query: bfloat16 [4, 1024, 8192], P('branch', 'seq'), may hold values from -150 to 150
- key_new: bfloat16 [4, 1024, 1024], P('branch', 'seq'), may hold values from -6 to 6
- value_new: bfloat16 [4, 1024, 1024], P('branch', 'seq'), may hold values from -18 to 18
- hist_key: bfloat16 [128, 1024], P('seq'), may hold values from -6 to 6
- hist_value: bfloat16 [128, 1024], P('seq'), may hold values from -18 to 18
- sib_source: int32 [4, 4], replicated, may hold values from 0 to 3, as said below
- sib_block: int32 [4, 4], replicated, may hold values from 0 to 3, as said below
- sib_mask: int32 [4, 4, 4], replicated, may hold values 0 or 1
Outputs:
- attended: bfloat16 [4, 1024, 8192], P('branch', 'seq')
Inputs may be any that keep to these rules, and one draw needn't show every extreme that they name: `sib_source`: never the reader itself. In every reader's list exactly 2 slots name one source and no source is named more than 2 times. `sib_block`: A reader lists no block of one source twice.
All inputs are finite; a program needn't handle non-finite values.
Results may differ from a plain program's by a relative error of at most 0.0036.
Values may be sent and summed in bfloat16 or wider, within the bound.
A program may use at most 128 MiB of HBM per device.

v0:
```python
import math

import jax
import jax.numpy as jnp
from jax import lax
from jax.sharding import PartitionSpec as P

QH = 64
KVH = 8
HD = 128
BLOCK = 256
NSIB = 4


def widen_devices(rows, seq_count):
    row_count = rows.shape[0]
    spread = jnp.broadcast_to(
        rows.reshape(row_count, KVH, 1, HD), (row_count, KVH, seq_count // KVH, HD)
    )
    return spread.reshape(row_count, seq_count, HD)


def visibility(first_row, tile_rows, own_length, hist_rows, mask_rows):
    positions = first_row + jnp.arange(tile_rows, dtype=jnp.int32)
    past = jnp.ones((tile_rows, hist_rows), dtype=jnp.bool_)
    causal = jnp.arange(own_length, dtype=jnp.int32)[None, :] <= positions[:, None]
    listed = jnp.repeat(mask_rows[positions // BLOCK] == 1, BLOCK, axis=1)
    return jnp.concatenate([past, causal, listed], axis=1)


def attend(head_q, all_keys, all_values, mask_rows, own_length, hist_rows):
    tile_rows = min(512, own_length)
    tile_count = own_length // tile_rows
    score_scale = 1.0 / math.sqrt(HD)

    def per_tile(tile_index):
        first_row = tile_index * tile_rows
        tile_q = lax.dynamic_slice_in_dim(head_q, first_row, tile_rows, 0)
        scores = (
            jnp.einsum("thd,kd->htk", tile_q, all_keys, preferred_element_type=jnp.float32)
            * score_scale
        )
        visible = visibility(first_row, tile_rows, own_length, hist_rows, mask_rows)
        scores = jnp.where(visible[None], scores, -jnp.inf)
        largest = jnp.max(scores, axis=-1, keepdims=True)
        weights = jnp.exp(scores - largest)
        weight_total = jnp.sum(weights, axis=-1)
        weight_bf = weights.astype(jnp.bfloat16)
        weighted = jnp.einsum(
            "htk,kd->thd", weight_bf, all_values, preferred_element_type=jnp.float32
        )
        return (weighted / weight_total.T[:, :, None]).astype(jnp.bfloat16)

    tiles = lax.map(per_tile, jnp.arange(tile_count, dtype=jnp.int32))
    return tiles.reshape(own_length, head_q.shape[1], HD)


def body(query, key_new, value_new, hist_key, hist_value, sib_source, sib_block, sib_mask):
    seq_count = lax.axis_size("seq")
    branch_count = lax.axis_size("branch")
    tok_local = query.shape[1]
    heads_local = QH // seq_count
    own_length = tok_local * seq_count
    block_count = own_length // BLOCK
    q_send = query.reshape(tok_local, seq_count, heads_local * HD)
    q_heads = lax.all_to_all(q_send, "seq", split_axis=1, concat_axis=0, tiled=True).reshape(
        own_length, heads_local, HD
    )
    own_k, own_v, past_k, past_v = (
        lax.all_to_all(
            widen_devices(key_new[0], seq_count), "seq", split_axis=1, concat_axis=0, tiled=True
        ),
        lax.all_to_all(
            widen_devices(value_new[0], seq_count), "seq", split_axis=1, concat_axis=0, tiled=True
        ),
        lax.all_to_all(
            widen_devices(hist_key, seq_count), "seq", split_axis=1, concat_axis=0, tiled=True
        ),
        lax.all_to_all(
            widen_devices(hist_value, seq_count), "seq", split_axis=1, concat_axis=0, tiled=True
        ),
    )
    own_k = own_k[:, 0, :]
    own_v = own_v[:, 0, :]
    past_k = past_k[:, 0, :]
    past_v = past_v[:, 0, :]
    reader = lax.axis_index("branch")
    my_source = lax.dynamic_index_in_dim(sib_source, reader, 0, keepdims=False)
    my_block = lax.dynamic_index_in_dim(sib_block, reader, 0, keepdims=False)
    my_mask = lax.dynamic_index_in_dim(sib_mask, reader, 0, keepdims=False)
    every_k, every_v = (
        lax.all_gather(own_k.reshape(1, block_count, BLOCK, HD), "branch", axis=0, tiled=True),
        lax.all_gather(own_v.reshape(1, block_count, BLOCK, HD), "branch", axis=0, tiled=True),
    )
    flat_index = my_source * block_count + my_block
    listed_k = every_k.reshape(branch_count * block_count, BLOCK, HD)[flat_index]
    listed_v = every_v.reshape(branch_count * block_count, BLOCK, HD)[flat_index]
    all_keys = jnp.concatenate([past_k, own_k, listed_k.reshape(NSIB * BLOCK, HD)], axis=0)
    all_values = jnp.concatenate([past_v, own_v, listed_v.reshape(NSIB * BLOCK, HD)], axis=0)
    result = attend(q_heads, all_keys, all_values, my_mask, own_length, past_k.shape[0])
    back_send = result.reshape(own_length, 1, heads_local * HD)
    returned = lax.all_to_all(back_send, "seq", split_axis=0, concat_axis=1, tiled=True)
    return returned.reshape(1, tok_local, QH * HD)


def solution(mesh):
    in_specs = (
        P("branch", "seq", None),
        P("branch", "seq", None),
        P("branch", "seq", None),
        P("seq", None),
        P("seq", None),
        P(),
        P(),
        P(),
    )
    out_specs = P("branch", "seq", None)
    return jax.shard_map(body, mesh=mesh, in_specs=in_specs, out_specs=out_specs, check_vma=False)
```

profile of v0, /device:TPU:9, one launch (start us, length us, event | category | flops | bytes accessed | tf_op | source)
XLA Modules:
  0.0 318.4 jit_solution(16479386253997616143)
XLA Ops:
  6.5 0.8 copy-done
  7.9 5.6 %all-to-all-start.1 = ((bf16[16,8,128]{2,0,1:T(8,128)(2,1)}), bf16[16,8,128]{2,0,1:T(8,128)(2,1)S(1)}, u32[]{:S(2)}, u32[]{:S(2)}) async-start(bf16[16,8,128]{2,0,1:T(8,128)(2,1)} %copy_bitcast_fusion.1), calls=%async_computation.1 | async-start | bytes 65536 | tf_op jit(solution)/shard_map/all_to_all | solution.py:76
  13.6 1.4 copy_bitcast_fusion
  14.9 2.6 all-to-all-done.1
  17.6 5.0 %all-to-all-start.3 = ((bf16[16,8,128]{2,0,1:T(8,128)(2,1)}), bf16[16,8,128]{2,0,1:T(8,128)(2,1)S(1)}, u32[]{:S(2)}, u32[]{:S(2)}) async-start(bf16[16,8,128]{2,0,1:T(8,128)(2,1)} %copy_bitcast_fusion), calls=%async_computation.3 | async-start | bytes 65536 | tf_op jit(solution)/shard_map/all_to_all | solution.py:79
  22.5 1.0 copy.48
  23.5 0.7 copy.31
  24.3 2.3 all-to-all-done.3
  26.6 5.1 %all-to-all-start.2 = ((bf16[128,8,128]{2,0,1:T(8,128)(2,1)}), bf16[128,8,128]{2,0,1:T(8,128)(2,1)S(1)}, u32[]{:S(2)}, u32[]{:S(2)}) async-start(bf16[128,8,128]{2,0,1:T(8,128)(2,1)} %copy.31), calls=%async_computation.2 | async-start | bytes 524288 | tf_op jit(solution)/shard_map/all_to_all | solution.py:70
  31.6 1.0 copy.49
  32.6 0.7 copy.33
  33.4 5.5 %all-to-all-done.2 = bf16[128,8,128]{2,0,1:T(8,128)(2,1)S(1)} async-done(((bf16[128,8,128]{2,0,1:T(8,128)(2,1)}), bf16[128,8,128]{2,0,1:T(8,128)(2,1)S(1)}, u32[]{:S(2)}, u32[]{:S(2)}) %all-to-all-start.2) | async-done | bytes 262176 | tf_op jit(solution)/shard_map/all_to_all | solution.py:70
  38.9 5.8 %all-to-all-start.4 = ((bf16[128,8,128]{2,0,1:T(8,128)(2,1)}), bf16[128,8,128]{2,0,1:T(8,128)(2,1)S(1)}, u32[]{:S(2)}, u32[]{:S(2)}) async-start(bf16[128,8,128]{2,0,1:T(8,128)(2,1)} %copy.33), calls=%async_computation.4 | async-start | bytes 524288 | tf_op jit(solution)/shard_map/all_to_all | solution.py:73
  45.4 1.4 copy.46
  46.9 2.5 copy.29
  49.3 2.6 all-to-all-done.4
  51.9 6.1 %all-to-all-start = ((bf16[128,8,1024]{2,0,1:T(8,128)(2,1)}), bf16[128,8,1024]{2,0,1:T(8,128)(2,1)S(1)}, u32[]{:S(2)}, u32[]{:S(2)}) async-start(bf16[128,8,1024]{2,0,1:T(8,128)(2,1)} %copy.29), calls=%async_computation | async-start | bytes 4194304 | tf_op jit(solution)/shard_map/all_to_all | solution.py:66
  58.0 0.7 all-gather.5.cloned.1.call-update
  58.8 0.7 fusion.20
  60.2 14.5 %all-gather.3.cloned.1.call-done = bf16[4,4,256,128]{3,2,1,0:T(8,128)(2,1)} async-done(((bf16[1,4,256,128]{3,2,1,0:T(8,128)(2,1)}), bf16[4,4,256,128]{3,2,1,0:T(8,128)(2,1)}) %all-gather.3.cloned.1.call-update) | async-done | bytes 1048592 | tf_op jit(solution)/shard_map/all_gather | solution.py:92
  74.7 1.8 gather_fusion.1
  76.5 26.7 %all-gather.5.cloned.1.call-done = bf16[4,4,256,128]{3,2,1,0:T(8,128)(2,1)} async-done(((bf16[1,4,256,128]{3,2,1,0:T(8,128)(2,1)}), bf16[4,4,256,128]{3,2,1,0:T(8,128)(2,1)}) %all-gather.5.cloned.1.call-update) | async-done | bytes 1048592 | tf_op jit(solution)/shard_map/all_gather | solution.py:93
  103.2 1.8 gather_fusion.2
  105.0 0.8 pad_maximum_fusion
  105.9 0.9 pad_maximum_fusion.1
  106.7 1.3 copy-done.5
  108.1 2.2 copy.47
  110.3 106.5 %while.12 = (s32[]{:T(128)}, bf16[2,512,8,128]{3,2,1,0:T(8,128)(2,1)}, s32[2]{0:T(128)S(1)}, s32[4,4]{1,0:T(4,128)S(1)}, bf16[1024,8,128]{2,1,0:T(8,128)(2,1)S(1...) while((s32[]{:T(128)}, ...), condition=%wide.region_3.4_spmd, body=%wide.region_0.3_spmd.sunk | while | flops 4665250816 | bytes 143326512 | solution.py:54
  111.9 1.0 gather_fusion
  113.0 1.6 broadcast_in_dim.74
  115.9 14.9 %bitcast_reduce_fusion.2 = (f32[8,512]{1,0:T(8,128)S(1)}, f32[512,8,2176]{2,0,1:T(8,128)}) fusion(pred[512,2176]{1,0:T(8,128)(4,1)S(1)} %pad_add_fusion.2, bf16[2176,128]{1,0:T(8,128)(2,1)S(1)} %copy-done.4, bf16[512,8,128]{2,1,0:T(8,128)(2,1)S(1)} %constant_dynamic-slice_fusion.4), kind=kOutput, calls=%fused_computation.4.clone.1 | convolution fusion | flops 2308435968 | bytes 38387712 | tf_op jit(solution)/shard_map/while/body/eval_jaxpr/thd,kd->htk/dot_general | solution.py:40
  130.8 15.7 %fusion.29 = f32[8,512]{1,0:T(8,128)S(1)} fusion(f32[512,8,2176]{2,0,1:T(8,128)} %get-tuple-element.178, f32[8,512]{1,0:T(8,128)S(1)} %get-tuple-element.179, pred[512,2176]{1,0:T(8,128)(4,1)S(1)} %pad_add_fusion.2), kind=kLoop, calls=%fused_computation.7.clone.1 | loop fusion | flops 35647488 | bytes 36798464 | tf_op jit(solution)/shard_map/while/body/eval_jaxpr/reduce_sum | solution.py:47
  146.5 15.5 %fusion.30 = bf16[1,512,8,128]{3,1,2,0:T(8,128)(2,1)S(1)} fusion(f32[512,8,2176]{2,0,1:T(8,128)} %get-tuple-element.178, f32[8,512]{1,0:T(8,128)S(1)} %get-tuple-element.179, pred[512,2176]{1,0:T(8,128)(4,1)S(1)} %pad_add_fusion.2, f32[512,8]{0,1:T(8,128)S(1)} %bitcast.142, bf16[2176,128]{1,0:T(8,128)(2,1)S(1)} %copy-done.11), kind=kOutput, calls=%fused_computation.15.clone.1 | convolution fusion | flops 2318401536 | bytes 38404096 | tf_op jit(solution)/shard_map/while/body/eval_jaxpr/htk,kd->thd/dot_general | solution.py:49
  162.0 1.7 copy_dynamic-update-slice_fusion.2
  165.1 1.0 gather_fusion
  166.2 1.6 broadcast_in_dim.74
  169.1 14.9 %bitcast_reduce_fusion.2 = (f32[8,512]{1,0:T(8,128)S(1)}, f32[512,8,2176]{2,0,1:T(8,128)}) fusion(pred[512,2176]{1,0:T(8,128)(4,1)S(1)} %pad_add_fusion.2, bf16[2176,128]{1,0:T(8,128)(2,1)S(1)} %copy-done.4, bf16[512,8,128]{2,1,0:T(8,128)(2,1)S(1)} %constant_dynamic-slice_fusion.4), kind=kOutput, calls=%fused_computation.4.clone.1 | convolution fusion | flops 2308435968 | bytes 38387712 | tf_op jit(solution)/shard_map/while/body/eval_jaxpr/thd,kd->htk/dot_general | solution.py:40
  183.9 15.7 %fusion.29 = f32[8,512]{1,0:T(8,128)S(1)} fusion(f32[512,8,2176]{2,0,1:T(8,128)} %get-tuple-element.178, f32[8,512]{1,0:T(8,128)S(1)} %get-tuple-element.179, pred[512,2176]{1,0:T(8,128)(4,1)S(1)} %pad_add_fusion.2), kind=kLoop, calls=%fused_computation.7.clone.1 | loop fusion | flops 35647488 | bytes 36798464 | tf_op jit(solution)/shard_map/while/body/eval_jaxpr/reduce_sum | solution.py:47
  199.7 15.5 %fusion.30 = bf16[1,512,8,128]{3,1,2,0:T(8,128)(2,1)S(1)} fusion(f32[512,8,2176]{2,0,1:T(8,128)} %get-tuple-element.178, f32[8,512]{1,0:T(8,128)S(1)} %get-tuple-element.179, pred[512,2176]{1,0:T(8,128)(4,1)S(1)} %pad_add_fusion.2, f32[512,8]{0,1:T(8,128)S(1)} %bitcast.142, bf16[2176,128]{1,0:T(8,128)(2,1)S(1)} %copy-done.11), kind=kOutput, calls=%fused_computation.15.clone.1 | convolution fusion | flops 2318401536 | bytes 38404096 | tf_op jit(solution)/shard_map/while/body/eval_jaxpr/htk,kd->thd/dot_general | solution.py:49
  215.2 1.7 copy_dynamic-update-slice_fusion.2
  216.8 12.5 %reshape_reshape.12 = bf16[1024,1,1024]{2,1,0:T(2,128)(2,1)} reshape(bf16[2,512,8,128]{3,2,1,0:T(8,128)(2,1)} %get-tuple-element.95) | data formatting | bytes 4194304 | tf_op jit(solution)/shard_map/reshape;reshape | solution.py:101
  229.8 12.8 %reduce = bf16[1024,1024]{1,0:T(8,128)(2,1)S(1)} reduce(bf16[1024,1,1024]{2,1,0:T(2,128)(2,1)} %reshape_reshape.12, bf16[]{:T(256)} %broadcast.199), dimensions={1}, to_apply=%reshape_reshape.12.reduce_sub_computation | reduce | bytes 4194306 | tf_op jit(solution)/shard_map/reshape;reshape | solution.py:101
  242.6 3.8 %reshape.168 = bf16[8,2,65536]{2,1,0:T(2,128)(2,1)} reshape(bf16[1024,1024]{1,0:T(8,128)(2,1)S(1)} %reduce) | data formatting | bytes 4194304
  246.4 51.4 %all_to_all.90 = bf16[8,2,65536]{2,1,0:T(2,128)(2,1)S(1)} all-to-all(bf16[8,2,65536]{2,1,0:T(2,128)(2,1)} %reshape.168), channel_id=1, replica_groups=mesh['branch'=4,'seq'=8] {'seq'}, dimensions={0} | all-to-all | bytes 4194304 | tf_op jit(solution)/shard_map/all_to_all | solution.py:102
  297.8 4.4 %reshape.169 = bf16[1024,1,1024]{2,1,0:T(2,128)(2,1)} reshape(bf16[8,2,65536]{2,1,0:T(2,128)(2,1)S(1)} %all_to_all.90) | data formatting | bytes 4194304
  302.1 3.0 copy.42
  305.1 2.4 copy.37
  307.5 4.1 %copy.38 = bf16[1,128,8192]{2,1,0:T(8,128)(2,1)} copy(bf16[1,128,8192]{1,2,0:T(8,128)(2,1)} %bitcast.131) | data formatting | bytes 4194304 | tf_op jit(solution)/shard_map/reshape | solution.py:103
  (62 shorter events, 6.6 us)
Async XLA Ops:
  6.5 0.8 copy-start
  6.5 38.9 %copy-start.10 = (bf16[1,128,8192]{2,1,0:T(8,128)(2,1)S(1)}, bf16[1,128,8192]{2,1,0:T(8,128)(2,1)}, u32[]{:S(2)}) copy-start(bf16[1,128,8192]{2,1,0:T(8,128)(2,1)} %param.10) | copy-start | bytes 6291460
  7.9 9.6 %all-to-all-start.1 = ((bf16[16,8,128]{2,0,1:T(8,128)(2,1)}), bf16[16,8,128]{2,0,1:T(8,128)(2,1)S(1)}, u32[]{:S(2)}, u32[]{:S(2)}) async-start(bf16[16,8,128]{2,0,1:T(8,128)(2,1)} %copy_bitcast_fusion.1), calls=%async_computation.1 | async-start | bytes 65536 | tf_op jit(solution)/shard_map/all_to_all | solution.py:76
  17.6 9.0 %all-to-all-start.3 = ((bf16[16,8,128]{2,0,1:T(8,128)(2,1)}), bf16[16,8,128]{2,0,1:T(8,128)(2,1)S(1)}, u32[]{:S(2)}, u32[]{:S(2)}) async-start(bf16[16,8,128]{2,0,1:T(8,128)(2,1)} %copy_bitcast_fusion), calls=%async_computation.3 | async-start | bytes 65536 | tf_op jit(solution)/shard_map/all_to_all | solution.py:79
  26.6 12.3 %all-to-all-start.2 = ((bf16[128,8,128]{2,0,1:T(8,128)(2,1)}), bf16[128,8,128]{2,0,1:T(8,128)(2,1)S(1)}, u32[]{:S(2)}, u32[]{:S(2)}) async-start(bf16[128,8,128]{2,0,1:T(8,128)(2,1)} %copy.31), calls=%async_computation.2 | async-start | bytes 524288 | tf_op jit(solution)/shard_map/all_to_all | solution.py:70
  38.9 5.9 %copy-start.6 = (bf16[128,8,128]{2,0,1:T(8,128)(2,1)}, bf16[128,8,128]{2,0,1:T(8,128)(2,1)S(1)}, u32[]{:S(2)}) copy-start(bf16[128,8,128]{2,0,1:T(8,128)(2,1)S(1)} %all-to-all-done.2) | copy-start | bytes 786436
  38.9 13.1 %all-to-all-start.4 = ((bf16[128,8,128]{2,0,1:T(8,128)(2,1)}), bf16[128,8,128]{2,0,1:T(8,128)(2,1)S(1)}, u32[]{:S(2)}, u32[]{:S(2)}) async-start(bf16[128,8,128]{2,0,1:T(8,128)(2,1)} %copy.33), calls=%async_computation.4 | async-start | bytes 524288 | tf_op jit(solution)/shard_map/all_to_all | solution.py:73
  44.7 30.0 %all-gather.3.cloned.1.call-start = ((), (), s32[]{:S(2)}) async-start(), calls=%async_computation.6 | async-start | bytes 1310720 | tf_op jit(solution)/shard_map/all_gather | solution.py:92
  49.3 55.7 %copy-start.7 = (bf16[128,8,128]{2,0,1:T(8,128)(2,1)S(1)}, bf16[128,8,128]{2,0,1:T(8,128)(2,1)}, u32[]{:S(2)}) copy-start(bf16[128,8,128]{2,0,1:T(8,128)(2,1)} %copy-done.6) | copy-start | bytes 786436
  51.9 6.1 %copy-start.8 = (bf16[128,8,128]{2,0,1:T(8,128)(2,1)}, bf16[128,8,128]{2,0,1:T(8,128)(2,1)S(1)}, u32[]{:S(2)}) copy-start(bf16[128,8,128]{2,0,1:T(8,128)(2,1)S(1)} %all-to-all-done.4) | copy-start | bytes 786436
  51.9 54.8 %all-to-all-start = ((bf16[128,8,1024]{2,0,1:T(8,128)(2,1)}), bf16[128,8,1024]{2,0,1:T(8,128)(2,1)S(1)}, u32[]{:S(2)}, u32[]{:S(2)}) async-start(bf16[128,8,1024]{2,0,1:T(8,128)(2,1)} %copy.29), calls=%async_computation | async-start | bytes 4194304 | tf_op jit(solution)/shard_map/all_to_all | solution.py:66
  58.0 45.2 %all-gather.5.cloned.1.call-start = ((), (), s32[]{:S(2)}) async-start(), calls=%async_computation.7 | async-start | bytes 1310720 | tf_op jit(solution)/shard_map/all_gather | solution.py:93
  58.0 47.8 %copy-start.9 = (bf16[128,8,128]{2,0,1:T(8,128)(2,1)S(1)}, bf16[128,8,128]{2,0,1:T(8,128)(2,1)}, u32[]{:S(2)}) copy-start(bf16[128,8,128]{2,0,1:T(8,128)(2,1)} %copy-done.8) | copy-start | bytes 786436
  106.7 1.3 copy-start.5
  110.5 1.5 copy-start.2
  113.0 2.9 copy-start.4
  130.8 15.7 %copy-start.11 = (bf16[2176,128]{1,0:T(8,128)(2,1)S(1)}, bf16[2176,128]{1,0:T(8,128)(2,1)}, u32[]{:S(2)}) copy-start(bf16[2176,128]{1,0:T(8,128)(2,1)} %get-tuple-element.212) | copy-start | bytes 1671172 | tf_op jit(solution)/shard_map/while
  162.0 1.7 copy-start.3
  163.6 1.5 copy-start.2
  166.2 2.9 copy-start.4
  183.9 15.7 %copy-start.11 = (bf16[2176,128]{1,0:T(8,128)(2,1)S(1)}, bf16[2176,128]{1,0:T(8,128)(2,1)}, u32[]{:S(2)}) copy-start(bf16[2176,128]{1,0:T(8,128)(2,1)} %get-tuple-element.212) | copy-start | bytes 1671172 | tf_op jit(solution)/shard_map/while
  215.1 1.7 copy-start.3
  307.5 4.1 %copy-start.1 = (bf16[16,1024]{1,0:T(8,128)(2,1)S(1)}, bf16[16,1024]{1,0:T(8,128)(2,1)}, u32[]{:S(2)}) copy-start(bf16[16,1024]{1,0:T(8,128)(2,1)} %param.13) | copy-start | bytes 98308
Sparse Core Ops, SparseCore 0:
  47.4 27.2 all-gather.2
  76.5 26.6 all-gather.4
where the time goes:
time: 324 us; the launch traced here: 318 us
  matrix products  60.7 us (19%)
  local copies, waits for them, and re-layouts  59.3 us (18%)
  waiting for transfers between devices  55.6 us (17%)
  blocking collectives  51.4 us (16%)
  other arithmetic  48.6 us (15%)
  starting transfers between devices  27.6 us (9%)
  between operations  13.5 us (4%)
    all_to_all x1, blocking collectives, body(): lax.all_to_all(back_send, 'seq', split_axis=0, concat_axis=1, tiled=True)  51.4 us
    reduce_sum x2, other arithmetic, per_tile(): weight_total = jnp.sum(weights, axis=-1)  31.4 us
    dot_general x2, matrix products, per_tile(): jnp.einsum('htk,kd->thd', weight_bf, all_values, preferred_element_type=j...  30.9 us
    dot_general x2, matrix products, per_tile(): jnp.einsum('thd,kd->htk', tile_q, all_keys, preferred_element_type=jnp.fl...  29.8 us
    all_gather x1, waiting for transfers between devices, body(): lax.all_gather(own_v.reshape(1, block_count, BLOCK, HD), 'branch', axis=0...  26.7 us
    unnamed x23, local copies, waits for them, and re-layouts  18.8 us
    all_gather x1, waiting for transfers between devices, body(): lax.all_gather(own_k.reshape(1, block_count, BLOCK, HD), 'branch', axis=0...  14.5 us
    another operation x2, local copies, waits for them, and re-layouts, body(): back_send = result.reshape(own_length, 1, heads_local * HD)  13 us
  transfers between devices with their start and end apart: 7, of which 6 were waited for; matrix products, arithmetic and copies ran while one was open for 5% of the time, Pallas kernels for 0%

commit v1 on v0

v1 whole, which is shorter than its diff:
```python
import functools
import math

import jax
import jax.numpy as jnp
from jax import lax
from jax.experimental import pallas as pl
from jax.experimental.pallas import tpu as pltpu
from jax.sharding import PartitionSpec as P

QH = 64
KVH = 8
HD = 128
BLOCK = 256
NSIB = 4
SRCMAX = 2
CORES = 2
GROUP = QH // KVH
HEADS = KVH // CORES
HIDDEN = -1e30
MESH = pl.DeviceIdType.MESH


def kernel(chips, branches, query, key_new, value_new, hist_key, hist_value, source, block, mask,
           out, qbuf, obuf, kv, pick, got, line_held, sib_held, keys, values, scores, bias,
           pair_local, pair_send, pair_recv, q_local, q_send, q_recv,
           line_send, line_recv, sib_send, sib_recv, o_local, o_send, o_recv):
    branch = lax.axis_index("branch")
    place = lax.axis_index("seq")
    chip = place // CORES
    core = place % CORES
    partner = (branch, chip * CORES + 1 - core)
    tokens = query.shape[1]
    hist_rows = hist_key.shape[0]
    hist_all = chips * CORES * hist_rows
    total = keys.shape[0]
    own_at = hist_all
    sib_at = hist_all + chips * BLOCK

    def line_device(step):
        return (branch, ((chip + step) % chips) * CORES + core)

    def sib_device(step):
        return ((branch + step) % branches, place)

    everyone = [partner]
    everyone += [line_device(step) for step in range(1, chips)]
    everyone += [sib_device(step) for step in range(1, branches)]
    barrier = pltpu.get_barrier_semaphore()
    for device in everyone:
        pl.semaphore_signal(barrier, inc=1, device_id=device, device_id_type=MESH)
    pl.semaphore_wait(barrier, len(everyone))

    my_rows = pl.ds(pl.multiple_of(core * tokens, tokens), tokens)
    other_rows = pl.ds(pl.multiple_of((1 - core) * tokens, tokens), tokens)
    my_hist = pl.ds(pl.multiple_of(BLOCK + core * hist_rows, hist_rows), hist_rows)

    def pair_parts(h, owner):
        cols = pl.ds(pl.multiple_of((owner * HEADS + h) * HD, HD), HD)
        return [
            (key_new.at[0, :, cols], kv.at[h, chip, 0, my_rows, :]),
            (value_new.at[0, :, cols], kv.at[h, chip, 1, my_rows, :]),
            (hist_key.at[:, cols], kv.at[h, chip, 0, my_hist, :]),
            (hist_value.at[:, cols], kv.at[h, chip, 1, my_hist, :]),
        ]

    def pair_copies(h):
        here = [
            pltpu.make_async_copy(src, dst, pair_local.at[h, n])
            for n, (src, dst) in enumerate(pair_parts(h, core))
        ]
        there = [
            pltpu.make_async_remote_copy(
                src_ref=src, dst_ref=dst, send_sem=pair_send.at[h, n], recv_sem=pair_recv.at[h, n],
                device_id=partner, device_id_type=MESH)
            for n, (src, dst) in enumerate(pair_parts(h, 1 - core))
        ]
        return here, there

    def q_copies(h):
        def cols(owner):
            return pl.ds(pl.multiple_of((owner * HEADS + h) * GROUP * HD, HD), GROUP * HD)

        here = pltpu.make_async_copy(
            query.at[0, :, cols(core)], qbuf.at[h, my_rows, :], q_local.at[h])
        there = pltpu.make_async_remote_copy(
            src_ref=query.at[0, :, cols(1 - core)], dst_ref=qbuf.at[h, my_rows, :],
            send_sem=q_send.at[h], recv_sem=q_recv.at[h], device_id=partner, device_id_type=MESH)
        return here, there

    def line_copy(h, step):
        return pltpu.make_async_remote_copy(
            src_ref=kv.at[h, chip], dst_ref=kv.at[h, chip],
            send_sem=line_send.at[h, step - 1], recv_sem=line_recv.at[h, step - 1],
            device_id=line_device(step), device_id_type=MESH)

    def sib_copy(h, step):
        return pltpu.make_async_remote_copy(
            src_ref=pick.at[h, step - 1], dst_ref=got.at[h, step - 1],
            send_sem=sib_send.at[h, step - 1], recv_sem=sib_recv.at[h, step - 1],
            device_id=sib_device(step), device_id_type=MESH)

    def o_copies(h):
        cols = pl.ds(pl.multiple_of((core * HEADS + h) * GROUP * HD, HD), GROUP * HD)
        here = pltpu.make_async_copy(obuf.at[h, my_rows, :], out.at[0, :, cols], o_local.at[h])
        there = pltpu.make_async_remote_copy(
            src_ref=obuf.at[h, other_rows, :], dst_ref=out.at[0, :, cols],
            send_sem=o_send.at[h], recv_sem=o_recv.at[h], device_id=partner, device_id_type=MESH)
        return here, there

    @pl.loop(0, HEADS)
    def _(h):
        here, there = pair_copies(h)
        for copy in there + here:
            copy.start()

    @pl.loop(0, HEADS)
    def _(h):
        here, there = pair_copies(h)
        for copy in here:
            copy.wait()
        for copy in there:
            copy.wait_recv()
        for step in range(1, chips):
            line_copy(h, step).start()

    @pl.loop(0, HEADS)
    def _(h):
        here, there = q_copies(h)
        there.start()
        here.start()

    bias[:, 0:hist_all] = jnp.zeros((BLOCK, hist_all), jnp.float32)
    row = lax.broadcasted_iota(jnp.int32, (BLOCK, BLOCK), 0)
    col = lax.broadcasted_iota(jnp.int32, (BLOCK, BLOCK), 1)
    for j in range(chips):
        seen = col + j * BLOCK <= row + chip * BLOCK
        bias[:, own_at + j * BLOCK : own_at + (j + 1) * BLOCK] = jnp.where(seen, 0.0, HIDDEN)
    for i in range(NSIB):
        seen = jnp.broadcast_to(mask[branch, chip, i], (BLOCK, BLOCK)) == 1
        bias[:, sib_at + i * BLOCK : sib_at + (i + 1) * BLOCK] = jnp.where(seen, 0.0, HIDDEN)

    def send_listed(h):
        for step in range(1, chips):
            line_copy(h, step).wait_recv()
        for j in range(chips):
            line_held[j] = kv[h, j, :, 0:BLOCK, :]
        for step in range(1, branches):
            reader = (branch + step) % branches
            count = jnp.int32(0)
            wanted = [jnp.int32(0)] * SRCMAX
            for i in range(NSIB):
                hit = source[reader, i] == branch
                for k in range(SRCMAX):
                    wanted[k] = jnp.where(hit & (count == k), block[reader, i], wanted[k])
                count = count + jnp.where(hit, 1, 0)
            for k in range(SRCMAX):
                pick[h, step - 1, k] = line_held[wanted[k]]
            sib_copy(h, step).start()

    def lay_out(h):
        rows = CORES * hist_rows
        for j in range(chips):
            for kind, whole in enumerate((keys, values)):
                whole[j * rows : (j + 1) * rows, :] = kv[h, j, kind, BLOCK : BLOCK + rows, :]
                whole[own_at + j * BLOCK : own_at + (j + 1) * BLOCK, :] = kv[h, j, kind, 0:BLOCK, :]
        for step in range(1, branches):
            for k in range(SRCMAX):
                sib_held[step - 1, k] = got[h, step - 1, k]
        for i in range(NSIB):
            mine = source[branch, i]
            step = (branch - mine + branches) % branches
            rank = jnp.int32(0)
            for earlier in range(i):
                rank = rank + jnp.where(source[branch, earlier] == mine, 1, 0)
            at = jnp.clip(step - 1, 0, branches - 2)
            rank = jnp.minimum(rank, SRCMAX - 1)
            for kind, whole in enumerate((keys, values)):
                whole[sib_at + i * BLOCK : sib_at + (i + 1) * BLOCK, :] = sib_held[at, rank, kind]

    pieces = [(0, hist_all)] + [(at, BLOCK) for at in range(own_at, total, BLOCK)]
    rate = 1.0 / math.sqrt(HD)

    def attend(h):
        @pl.loop(0, GROUP)
        def _(g):
            cols = pl.ds(pl.multiple_of(g * HD, HD), HD)
            q = qbuf[h, :, cols]
            largest = None
            for at, width in pieces:
                s = lax.dot_general(
                    q, keys[at : at + width, :], (((1,), (1,)), ((), ())),
                    preferred_element_type=jnp.float32)
                s = s + bias[:, at : at + width]
                scores[:, at : at + width] = s
                for lane in range(0, width, HD):
                    part = s[:, lane : lane + HD]
                    largest = part if largest is None else jnp.maximum(largest, part)
            top = jnp.max(largest, axis=1, keepdims=True)
            summed = jnp.zeros((BLOCK, HD), jnp.float32)
            acc = jnp.zeros((BLOCK, HD), jnp.float32)
            for at, width in pieces:
                w = jnp.exp((scores[:, at : at + width] - top) * rate)
                for lane in range(0, width, HD):
                    summed = summed + w[:, lane : lane + HD]
                acc = acc + jnp.dot(
                    w.astype(jnp.bfloat16), values[at : at + width, :],
                    preferred_element_type=jnp.float32)
            weight_total = jnp.sum(summed, axis=1, keepdims=True)
            obuf[h, :, cols] = (acc / weight_total).astype(jnp.bfloat16)

    send_listed(0)

    @pl.loop(0, HEADS)
    def _(h):
        @pl.when(h + 1 < HEADS)
        def _():
            send_listed(h + 1)

        here, there = q_copies(h)
        here.wait()
        there.wait_recv()
        for step in range(1, branches):
            sib_copy(h, step).wait_recv()
        lay_out(h)
        attend(h)
        here, there = o_copies(h)
        there.start()
        here.start()

    @pl.loop(0, HEADS)
    def _(h):
        for copy in pair_copies(h)[1]:
            copy.wait_send()
        q_copies(h)[1].wait_send()
        for step in range(1, chips):
            line_copy(h, step).wait_send()
        for step in range(1, branches):
            sib_copy(h, step).wait_send()
        here, there = o_copies(h)
        here.wait()
        there.wait()


def body(query, key_new, value_new, hist_key, hist_value, sib_source, sib_block, sib_mask):
    chips = lax.axis_size("seq") // CORES
    branches = lax.axis_size("branch")
    hist_rows = hist_key.shape[0]
    hist_all = hist_rows * chips * CORES
    total = hist_all + chips * BLOCK + NSIB * BLOCK
    dma = pltpu.SemaphoreType.DMA
    anywhere = pl.BlockSpec(memory_space=pl.ANY)
    scalars = pl.BlockSpec(memory_space=pltpu.SMEM)
    return pl.pallas_call(
        functools.partial(kernel, chips, branches),
        out_shape=jax.ShapeDtypeStruct(query.shape, jnp.bfloat16),
        in_specs=[anywhere] * 5 + [scalars] * 3,
        out_specs=anywhere,
        scratch_shapes=[
            pltpu.VMEM((HEADS, BLOCK, GROUP * HD), jnp.bfloat16),
            pltpu.VMEM((HEADS, BLOCK, GROUP * HD), jnp.bfloat16),
            pltpu.VMEM((HEADS, chips, 2, BLOCK + CORES * hist_rows, HD), jnp.bfloat16),
            pltpu.VMEM((HEADS, branches - 1, SRCMAX, 2, BLOCK, HD), jnp.bfloat16),
            pltpu.VMEM((HEADS, branches - 1, SRCMAX, 2, BLOCK, HD), jnp.bfloat16),
            pltpu.VMEM((chips, 2, BLOCK, HD), jnp.bfloat16),
            pltpu.VMEM((branches - 1, SRCMAX, 2, BLOCK, HD), jnp.bfloat16),
            pltpu.VMEM((total, HD), jnp.bfloat16),
            pltpu.VMEM((total, HD), jnp.bfloat16),
            pltpu.VMEM((BLOCK, total), jnp.float32),
            pltpu.VMEM((BLOCK, total), jnp.float32),
            dma((HEADS, 4)), dma((HEADS, 4)), dma((HEADS, 4)),
            dma((HEADS,)), dma((HEADS,)), dma((HEADS,)),
            dma((HEADS, chips - 1)), dma((HEADS, chips - 1)),
            dma((HEADS, branches - 1)), dma((HEADS, branches - 1)),
            dma((HEADS,)), dma((HEADS,)), dma((HEADS,)),
        ],
        compiler_params=pltpu.CompilerParams(
            collective_id=0, has_side_effects=True, vmem_limit_bytes=56 * 1024 * 1024),
        cost_estimate=pl.CostEstimate(
            flops=4 * HEADS * GROUP * BLOCK * total * HD,
            bytes_accessed=2 * query.size * 2, transcendentals=HEADS * GROUP * BLOCK * total),
    )(query, key_new, value_new, hist_key, hist_value, sib_source, sib_block, sib_mask)


def solution(mesh):
    in_specs = (
        P("branch", "seq", None),
        P("branch", "seq", None),
        P("branch", "seq", None),
        P("seq", None),
        P("seq", None),
        P(),
        P(),
        P(),
    )
    out_specs = P("branch", "seq", None)
    return jax.shard_map(body, mesh=mesh, in_specs=in_specs, out_specs=out_specs, check_vma=False)
```

time: 324 us -> 100 us (0.31); the launches traced: 318 us -> 99.8 us
  Pallas kernels: 0 us -> 96.6 us
  matrix products: 60.7 us -> 0 us
  local copies, waits for them, and re-layouts: 59.3 us -> 3.1 us
  waiting for transfers between devices: 55.6 us -> 0 us
  blocking collectives: 51.4 us -> 0 us
  other arithmetic: 48.6 us -> 0 us
  starting transfers between devices: 27.6 us -> 0 us
  between operations: 13.5 us -> 0.01 us
    pallas_call x0 -> x1, Pallas kernels: none -> 96.6 us  [body(): pl.pallas_call(functools.partial(kernel, chips, branches), out_shape=jax....]
    dot_general x4 -> x0, matrix products: 60.7 us -> none  [the longest x2 30.9 us: per_tile(): jnp.einsum('htk,kd->thd', weight_bf, all_values, preferred_element_type=j...]
    all_to_all x1 -> x0, blocking collectives: 51.4 us -> none  [body(): lax.all_to_all(back_send, 'seq', split_axis=0, concat_axis=1, tiled=True)]
    all_gather x2 -> x0, waiting for transfers between devices: 41.2 us -> none  [the longest x1 26.7 us: body(): lax.all_gather(own_v.reshape(1, block_count, BLOCK, HD), 'branch', axis=0...]
    reduce_sum x2 -> x0, other arithmetic: 31.4 us -> none  [per_tile(): weight_total = jnp.sum(weights, axis=-1)]
    all_to_all x5 -> x0, starting transfers between devices: 27.6 us -> none  [the longest x1 6.06 us: body(): lax.all_to_all(q_send, 'seq', split_axis=1, concat_axis=0, tiled=True)]
    another operation x8 -> x0, local copies, waits for them, and re-layouts: 16.5 us -> none  [the longest x2 13 us: body(): back_send = result.reshape(own_length, 1, heads_local * HD)]
    unnamed x23 -> x1, local copies, waits for them, and re-layouts: 18.8 us -> 3.1 us
  transfers between devices with their start and end apart: 7 -> 0, of which waited for: 6 -> 0; matrix products, arithmetic and copies ran while one was open for 5% -> 0% of each run, Pallas kernels for 0% -> 0%
where the time goes in v1:
time: 100 us; the launch traced here: 99.8 us
  Pallas kernels  96.6 us (97%)
  local copies, waits for them, and re-layouts  3.1 us (3%)
    pallas_call x1, Pallas kernels, body(): pl.pallas_call(functools.partial(kernel, chips, branches), out_shape=jax....  96.6 us
    unnamed x1, local copies, waits for them, and re-layouts  3.1 us

profile of v1, /device:TPU:9, one launch (start us, length us, event | category | flops | bytes accessed | tf_op | source)
XLA Modules:
  0.0 99.8 jit_solution(9479317009531943522)
XLA Ops:
  0.0 96.6 %shard_map.82 = bf16[1,128,8192]{2,1,0:T(8,128)(2,1)} custom-call(bf16[1,128,8192]{2,1,0:T(8,128)(2,1)} %query.1, bf16[1,128,1024]{2,1,0:T(8,128)(2,1)} %key_new.1, bf16[1,128,1024]{2,1,0:T(8,128)(2,1)} %value_new.1, bf16[16,1024]{1,0:T(8,128)(2,1)} %hist_key.1, bf16[16,1024]{1,0:T(8,128)(2,1)} %hist_value.1, s32[4,4]{1,0:T(4,128)} %source.1, s32[4,4]{1,0:T(4,128)} %block.1, ...), custom_call_target="tpu_custom_call" | custom-call | flops 9126805504 | bytes 4194304 | tf_op jit(solution)/shard_map/pallas_call | solution.py:254
  96.7 3.1 %copy.10 = bf16[1,128,8192]{2,1,0:T(8,128)(2,1)} copy(bf16[1,128,8192]{2,1,0:T(8,128)(2,1)} %shard_map.82) | data formatting | bytes 4194304

commit v2 on v1

--- a/solution.py
+++ b/solution.py
@@ -23,6 +23,7 @@
 
 def kernel(chips, branches, query, key_new, value_new, hist_key, hist_value, source, block, mask,
            out, qbuf, obuf, kv, pick, got, line_held, sib_held, keys, values, scores, bias,
+           tops, sums, accs,
            pair_local, pair_send, pair_recv, q_local, q_send, q_recv,
            line_send, line_recv, sib_send, sib_recv, o_local, o_send, o_recv):
     branch = lax.axis_index("branch")
@@ -121,8 +122,11 @@
             copy.wait()
         for copy in there:
             copy.wait_recv()
-        for step in range(1, chips):
-            line_copy(h, step).start()
+
+        @pl.when(h == 0)
+        def _():
+            for step in range(1, chips):
+                line_copy(h, step).start()
 
     @pl.loop(0, HEADS)
     def _(h):
@@ -130,15 +134,19 @@
         there.start()
         here.start()
 
-    bias[:, 0:hist_all] = jnp.zeros((BLOCK, hist_all), jnp.float32)
     row = lax.broadcasted_iota(jnp.int32, (BLOCK, BLOCK), 0)
     col = lax.broadcasted_iota(jnp.int32, (BLOCK, BLOCK), 1)
     for j in range(chips):
         seen = col + j * BLOCK <= row + chip * BLOCK
-        bias[:, own_at + j * BLOCK : own_at + (j + 1) * BLOCK] = jnp.where(seen, 0.0, HIDDEN)
-    for i in range(NSIB):
-        seen = jnp.broadcast_to(mask[branch, chip, i], (BLOCK, BLOCK)) == 1
-        bias[:, sib_at + i * BLOCK : sib_at + (i + 1) * BLOCK] = jnp.where(seen, 0.0, HIDDEN)
+        bias[:, j * BLOCK : (j + 1) * BLOCK] = jnp.where(seen, 0.0, HIDDEN)
+
+    def send_line(h):
+        for step in range(1, chips):
+            line_copy(h, step).start()
+
+    def line_left(h):
+        for step in range(1, chips):
+            line_copy(h, step).wait_send()
 
     def send_listed(h):
         for step in range(1, chips):
@@ -158,12 +166,14 @@
                 pick[h, step - 1, k] = line_held[wanted[k]]
             sib_copy(h, step).start()
 
-    def lay_out(h):
+    def lay_out_own(h):
         rows = CORES * hist_rows
         for j in range(chips):
             for kind, whole in enumerate((keys, values)):
                 whole[j * rows : (j + 1) * rows, :] = kv[h, j, kind, BLOCK : BLOCK + rows, :]
                 whole[own_at + j * BLOCK : own_at + (j + 1) * BLOCK, :] = kv[h, j, kind, 0:BLOCK, :]
+
+    def lay_out_listed(h):
         for step in range(1, branches):
             for k in range(SRCMAX):
                 sib_held[step - 1, k] = got[h, step - 1, k]
@@ -178,52 +188,86 @@
             for kind, whole in enumerate((keys, values)):
                 whole[sib_at + i * BLOCK : sib_at + (i + 1) * BLOCK, :] = sib_held[at, rank, kind]
 
-    pieces = [(0, hist_all)] + [(at, BLOCK) for at in range(own_at, total, BLOCK)]
-    rate = 1.0 / math.sqrt(HD)
-
-    def attend(h):
+    own_pieces = [(0, hist_all)] + [(at, BLOCK) for at in range(own_at, sib_at, BLOCK)]
+    sib_pieces = [(at, BLOCK) for at in range(sib_at, total, BLOCK)]
+    rate = math.log2(math.e) / math.sqrt(HD)
+    shown = [jnp.where(mask[branch, chip, i] == 1, 0.0, HIDDEN) for i in range(NSIB)]
+
+    def score(q, pieces, largest):
+        for at, width in pieces:
+            s = lax.dot_general(
+                q, keys[at : at + width, :], (((1,), (1,)), ((), ())),
+                preferred_element_type=jnp.float32)
+            if at >= sib_at:
+                s = s + shown[(at - sib_at) // BLOCK]
+            elif at >= own_at:
+                s = s + bias[:, at - own_at : at - own_at + width]
+            scores[:, at : at + width] = s
+            for lane in range(0, width, HD):
+                part = s[:, lane : lane + HD]
+                largest = part if largest is None else jnp.maximum(largest, part)
+        return largest
+
+    def weigh(pieces, top, summed, acc):
+        for at, width in pieces:
+            w = jnp.exp2((scores[:, at : at + width] - top) * rate)
+            for lane in range(0, width, HD):
+                summed = summed + w[:, lane : lane + HD]
+            acc = acc + jnp.dot(
+                w.astype(jnp.bfloat16), values[at : at + width, :],
+                preferred_element_type=jnp.float32)
+        return summed, acc
+
+    def attend_own(h):
+        @pl.loop(0, GROUP)
+        def _(g):
+            q = qbuf[h, :, pl.ds(pl.multiple_of(g * HD, HD), HD)]
+            largest = score(q, own_pieces, None)
+            top = jnp.max(largest, axis=1, keepdims=True)
+            zero = jnp.zeros((BLOCK, HD), jnp.float32)
+            summed, acc = weigh(own_pieces, top, zero, zero)
+            tops[g] = jnp.broadcast_to(top, (BLOCK, HD))
+            sums[g] = summed
+            accs[g] = acc
+
+    def attend_listed(h):
         @pl.loop(0, GROUP)
         def _(g):
             cols = pl.ds(pl.multiple_of(g * HD, HD), HD)
-            q = qbuf[h, :, cols]
-            largest = None
-            for at, width in pieces:
-                s = lax.dot_general(
-                    q, keys[at : at + width, :], (((1,), (1,)), ((), ())),
-                    preferred_element_type=jnp.float32)
-                s = s + bias[:, at : at + width]
-                scores[:, at : at + width] = s
-                for lane in range(0, width, HD):
-                    part = s[:, lane : lane + HD]
-                    largest = part if largest is None else jnp.maximum(largest, part)
+            before = tops[g]
+            largest = score(qbuf[h, :, cols], sib_pieces, before)
             top = jnp.max(largest, axis=1, keepdims=True)
-            summed = jnp.zeros((BLOCK, HD), jnp.float32)
-            acc = jnp.zeros((BLOCK, HD), jnp.float32)
-            for at, width in pieces:
-                w = jnp.exp((scores[:, at : at + width] - top) * rate)
-                for lane in range(0, width, HD):
-                    summed = summed + w[:, lane : lane + HD]
-                acc = acc + jnp.dot(
-                    w.astype(jnp.bfloat16), values[at : at + width, :],
-                    preferred_element_type=jnp.float32)
+            shrink = jnp.exp2((before - top) * rate)
+            summed, acc = weigh(sib_pieces, top, sums[g] * shrink, accs[g] * shrink)
             weight_total = jnp.sum(summed, axis=1, keepdims=True)
             obuf[h, :, cols] = (acc / weight_total).astype(jnp.bfloat16)
 
+    line_left(0)
+    send_line(1)
     send_listed(0)
 
     @pl.loop(0, HEADS)
     def _(h):
-        @pl.when(h + 1 < HEADS)
-        def _():
-            send_listed(h + 1)
-
         here, there = q_copies(h)
         here.wait()
         there.wait_recv()
+        lay_out_own(h)
+        attend_own(h)
+
+        @pl.when(h + 1 < HEADS)
+        def _():
+            line_left(h + 1)
+
+            @pl.when(h + 2 < HEADS)
+            def _():
+                send_line(h + 2)
+
+            send_listed(h + 1)
+
         for step in range(1, branches):
             sib_copy(h, step).wait_recv()
-        lay_out(h)
-        attend(h)
+        lay_out_listed(h)
+        attend_listed(h)
         here, there = o_copies(h)
         there.start()
         here.start()
@@ -233,8 +277,6 @@
         for copy in pair_copies(h)[1]:
             copy.wait_send()
         q_copies(h)[1].wait_send()
-        for step in range(1, chips):
-            line_copy(h, step).wait_send()
         for step in range(1, branches):
             sib_copy(h, step).wait_send()
         here, there = o_copies(h)
@@ -267,7 +309,10 @@
             pltpu.VMEM((total, HD), jnp.bfloat16),
             pltpu.VMEM((total, HD), jnp.bfloat16),
             pltpu.VMEM((BLOCK, total), jnp.float32),
-            pltpu.VMEM((BLOCK, total), jnp.float32),
+            pltpu.VMEM((BLOCK, chips * BLOCK), jnp.float32),
+            pltpu.VMEM((GROUP, BLOCK, HD), jnp.float32),
+            pltpu.VMEM((GROUP, BLOCK, HD), jnp.float32),
+            pltpu.VMEM((GROUP, BLOCK, HD), jnp.float32),
             dma((HEADS, 4)), dma((HEADS, 4)), dma((HEADS, 4)),
             dma((HEADS,)), dma((HEADS,)), dma((HEADS,)),
             dma((HEADS, chips - 1)), dma((HEADS, chips - 1)),

time: 100 us -> 88.8 us (0.89)
  Pallas kernels: 96.6 us -> 85.3 us
    pallas_call x1, Pallas kernels: 96.6 us -> 85.3 us  [body(): pl.pallas_call(functools.partial(kernel, chips, branches), out_shape=jax....]
where the time goes in v2:
time: 88.8 us; the launch traced here: 88.4 us
  Pallas kernels  85.3 us (96%)
  local copies, waits for them, and re-layouts  3.1 us (3%)
    pallas_call x1, Pallas kernels, body(): pl.pallas_call(functools.partial(kernel, chips, branches), out_shape=jax....  85.3 us
    unnamed x1, local copies, waits for them, and re-layouts  3.1 us

profile of v2, /device:TPU:9, one launch (start us, length us, event | category | flops | bytes accessed | tf_op | source)
XLA Modules:
  0.0 88.4 jit_solution(17519088249208694499)
XLA Ops:
  0.0 85.3 %shard_map.82 = bf16[1,128,8192]{2,1,0:T(8,128)(2,1)} custom-call(bf16[1,128,8192]{2,1,0:T(8,128)(2,1)} %query.1, bf16[1,128,1024]{2,1,0:T(8,128)(2,1)} %key_new.1, bf16[1,128,1024]{2,1,0:T(8,128)(2,1)} %value_new.1, bf16[16,1024]{1,0:T(8,128)(2,1)} %hist_key.1, bf16[16,1024]{1,0:T(8,128)(2,1)} %hist_value.1, s32[4,4]{1,0:T(4,128)} %source.1, s32[4,4]{1,0:T(4,128)} %block.1, ...), custom_call_target="tpu_custom_call" | custom-call | flops 9126805504 | bytes 4194304 | tf_op jit(solution)/shard_map/pallas_call | solution.py:296
  85.3 3.1 %copy.10 = bf16[1,128,8192]{2,1,0:T(8,128)(2,1)} copy(bf16[1,128,8192]{2,1,0:T(8,128)(2,1)} %shard_map.82) | data formatting | bytes 4194304
